TPU v7x, 256 devices: a whole 4x4x8 slice. The times are simulated.
256 devices in a mesh: section: 16 (over y, x), expert: 4 (over z_lo, core), dp: 4 (over z_hi).
Axes of the slice: x: 4, y: 4, z: 8 (z_hi: 4, z_lo: 2; z = z_hi * 2 + z_lo), core: 2. Of those that a mesh axis runs over, the one named last changes fastest.
Arguments:
- x_now: bfloat16 [16, 2048, 3072], P('section', ('expert', 'dp')), may hold values from -6 to 6
- ids_now: int32 [16, 2048, 4], P('section', ('expert', 'dp')), may hold values from 0 to 15, as said below
- gates_now: float32 [16, 2048, 4], P('section', ('expert', 'dp')), may hold values from 0.05 to 1
- hidden_now: bfloat16 [16, 512, 6144], P('section', ('expert', 'dp')), may hold values from -6 to 6
- x_old: bfloat16 [16, 2048, 3072], P('section', ('expert', 'dp')), may hold values from -6 to 6
- ids_old: int32 [16, 2048, 4], P('section', ('expert', 'dp')), may hold values from 0 to 15, as said below
- gate_grad_old: bfloat16 [16, 512, 6144], P('section', None, ('expert', 'dp')), may hold values from -2 to 2
- up_grad_old: bfloat16 [16, 512, 6144], P('section', None, ('expert', 'dp')), may hold values from -2 to 2
- w_gate: bfloat16 [16, 3072, 6144], P('section', None, ('expert', 'dp')), may hold values from -0.109375 to 0.109375
- w_up: bfloat16 [16, 3072, 6144], P('section', None, ('expert', 'dp')), may hold values from -0.109375 to 0.109375
Outputs:
- passed_grad: bfloat16 [16, 2048, 3072], P('section', ('expert', 'dp'))
- dw_gate: bfloat16 [16, 3072, 6144], P('section', None, ('expert', 'dp'))
- dw_up: bfloat16 [16, 3072, 6144], P('section', None, ('expert', 'dp'))
Inputs may be any that keep to these rules, and one draw needn't show every extreme that they name: `ids_now`: each token names 4 different experts. In section s, at most 32 tokens of one aligned block of 128 name expert s mod 16; in every section some block has exactly 32 such tokens, and in some section every block has. `ids_old`: as for ids_now.
All inputs are finite; a program needn't handle non-finite values.
Results may differ from a plain program's by a relative error of at most 0.005.
Values may be sent and summed in bfloat16 or wider, within the bound.
A program may use at most 128 MiB of HBM per device.

v0:
```python
import jax
import jax.numpy as jnp
from jax import lax
from jax.sharding import PartitionSpec as P

EXPERTS = 16


def from_behind(array, axis, by):
    devices = lax.axis_size(axis)
    pairs = [(i, i + by) for i in range(devices) if 0 <= i + by < devices]
    return lax.ppermute(array, axis, pairs)


def pack_rows(tokens, ids, expert, capacity):
    hits = (ids == expert).astype(jnp.int32)
    routed = jnp.sum(hits, axis=1)
    slot = jnp.cumsum(routed) - routed
    places = jnp.arange(capacity, dtype=jnp.int32)
    table = ((slot[None, :] == places[:, None]) & (routed[None, :] == 1)).astype(jnp.float32)
    packed = jnp.dot(table.astype(jnp.bfloat16), tokens, preferred_element_type=jnp.float32).astype(
        jnp.bfloat16
    )
    return (table, packed, hits)


def shards(
    x_now, ids_now, gates_now, hidden_now, x_old, ids_old, gate_grad_old, up_grad_old, w_gate, w_up
):
    capacity = hidden_now.shape[1]
    expert = lax.axis_index("section") % EXPERTS
    table, packed, hits = pack_rows(x_now[0], ids_now[0], expert, capacity)
    weight_tok = jnp.sum(gates_now[0] * hits.astype(jnp.float32), axis=1)
    coef = jnp.sum(table * weight_tok[None, :], axis=1)
    old_table, packed_old, old_hits = pack_rows(x_old[0], ids_old[0], expert, capacity)
    gate_w = w_gate[0]
    up_w = w_up[0]
    width = gate_w.shape[1]
    stored = jnp.concatenate([gate_grad_old[0], up_grad_old[0]], axis=1)
    rows_dims = (((0,), (0,)), ((), ()))
    piece = lax.all_gather(packed, ("expert", "dp"), axis=0, tiled=True)
    gate_part = jnp.dot(piece, gate_w, preferred_element_type=jnp.float32)
    up_part = jnp.dot(piece, up_w, preferred_element_type=jnp.float32)
    projected = jnp.concatenate([gate_part, up_part], axis=1)
    weight_sum = lax.dot_general(
        lax.all_gather(packed_old, ("expert", "dp"), axis=0, tiled=True),
        stored,
        rows_dims,
        preferred_element_type=jnp.float32,
    )
    incoming = lax.all_to_all(
        hidden_now[0], ("expert", "dp"), split_axis=1, concat_axis=0, tiled=True
    ).astype(jnp.float32)
    gate = projected[:, :width]
    up = projected[:, width:]
    sig = jax.nn.sigmoid(gate)
    act = gate * sig
    slope = sig * (1.0 + gate * (1.0 - sig))
    gate_grad = (incoming * up * slope).astype(jnp.bfloat16)
    up_grad = (incoming * act).astype(jnp.bfloat16)
    feature_dims = (((1,), (1,)), ((), ()))
    term = lax.dot_general(gate_grad, gate_w, feature_dims, preferred_element_type=jnp.float32)
    summed = lax.psum_scatter(
        term + lax.dot_general(up_grad, up_w, feature_dims, preferred_element_type=jnp.float32),
        ("expert", "dp"),
        scatter_dimension=0,
        tiled=True,
    )
    packed_grad = (coef[:, None] * summed).astype(jnp.bfloat16)
    token_grad = lax.dot_general(
        table.astype(jnp.bfloat16), packed_grad, rows_dims, preferred_element_type=jnp.float32
    ).astype(jnp.bfloat16)
    passed_grad = from_behind(token_grad[None], "section", -1)
    dw_gate = weight_sum[:, :width].astype(jnp.bfloat16)[None]
    dw_up = weight_sum[:, width:].astype(jnp.bfloat16)[None]
    return (passed_grad, dw_gate, dw_up)


def solution(mesh):
    in_specs = (
        P("section", ("expert", "dp"), None),
        P("section", ("expert", "dp"), None),
        P("section", ("expert", "dp"), None),
        P("section", ("expert", "dp"), None),
        P("section", ("expert", "dp"), None),
        P("section", ("expert", "dp"), None),
        P("section", None, ("expert", "dp")),
        P("section", None, ("expert", "dp")),
        P("section", None, ("expert", "dp")),
        P("section", None, ("expert", "dp")),
    )
    out_specs = (
        P("section", ("expert", "dp"), None),
        P("section", None, ("expert", "dp")),
        P("section", None, ("expert", "dp")),
    )
    return jax.shard_map(shards, mesh=mesh, in_specs=in_specs, out_specs=out_specs, check_vma=False)
```

profile of v0, /device:TPU:30, one launch (start us, length us, event | category | flops | bytes accessed | tf_op | source)
XLA Modules:
  0.0 369.4 jit_solution(5260174058634829698)
XLA Ops:
  7.2 0.9 fusion.40
  8.2 0.1 copy.19
  8.3 0.2 reduce-window.16
  8.5 0.1 reduce.3
  8.6 2.1 convolution_convert_fusion.3
  10.7 0.7 convert_reduce_fusion.1
  11.4 0.1 copy.21
  11.5 0.2 reduce-window.17
  11.7 0.1 reduce.4
  11.8 2.1 convolution_convert_fusion.2
  14.1 26.9 %all_to_all.13 = bf16[32,16,384]{2,0,1:T(8,128)(2,1)S(1)} all-to-all(bf16[32,16,384]{2,0,1:T(8,128)(2,1)S(1)} %copy.20), channel_id=1, replica_groups=mesh['section'=16,'expert'=4,'dp'=4] {'expert','dp'}, dimensions={1} | all-to-all | bytes 786432 | tf_op jit(solution)/shard_map/all_to_all | solution.py:51
  41.1 64.9 %all-gather.3.cloned.1.call-done = bf16[512,3072]{1,0:T(8,128)(2,1)} async-done(((bf16[32,3072]{1,0:T(8,128)(2,1)}), bf16[512,3072]{1,0:T(8,128)(2,1)}) %all-gather.3.cloned.1.call-update) | async-done | bytes 3145744 | tf_op jit(solution)/shard_map/all_gather | solution.py:41
  106.0 5.4 %fusion.23 = (bf16[512,384]{1,0:T(8,128)(2,1)}, f32[512,384]{1,0:T(8,128)}) fusion(bf16[32,16,384]{2,0,1:T(8,128)(2,1)S(1)} %all_to_all.13, bf16[512,3072]{1,0:T(8,128)(2,1)} %all-gather.3.cloned.1.call-done, bf16[1,3072,384]{2,1,0:T(8,128)(2,1)} %param.18), kind=kOutput, calls=%fused_computation.23 | convolution fusion | flops 1209335808 | bytes 7077888 | tf_op jit(solution)/shard_map/dot_general | solution.py:42
  111.5 9.1 %fusion.1 = f32[512,3072]{1,0:T(8,128)} fusion(bf16[1,3072,384]{2,1,0:T(8,128)(2,1)} %param.18, f32[512,384]{1,0:T(8,128)S(1)} %bitcast.50, bf16[512,3072]{1,0:T(8,128)(2,1)} %all-gather.3.cloned.1.call-done, bf16[1,3072,384]{2,1,0:T(8,128)(2,1)S(1)} %copy-done, f32[512,384]{1,0:T(8,128)} %get-tuple-element.8), kind=kOutput, calls=%fused_computation.8 | convolution fusion | flops 2417885184 | bytes 15728640 | tf_op jit(solution)/shard_map/dot_general | solution.py:62
  120.6 7.3 %convolution_add_fusion = f32[512,3072]{1,0:T(8,128)} fusion(f32[512,3072]{1,0:T(8,128)} %fusion.1, bf16[512,384]{1,0:T(8,128)(2,1)S(1)} %copy-done.2, bf16[1,3072,384]{2,1,0:T(8,128)(2,1)S(1)} %copy-done), kind=kOutput, calls=%fused_computation.1 | convolution fusion | flops 1209532416 | bytes 15335424 | tf_op jit(solution)/shard_map/dot_general | solution.py:64
  127.9 0.1 select_reduce_fusion
  128.0 68.2 %all-gather.5.cloned.1.call-done = bf16[512,3072]{1,0:T(8,128)(2,1)} async-done(((bf16[32,3072]{1,0:T(8,128)(2,1)}), bf16[512,3072]{1,0:T(8,128)(2,1)}) %all-gather.5.cloned.1.call-update) | async-done | bytes 3145744 | tf_op jit(solution)/shard_map/all_gather | solution.py:46
  196.3 6.8 %convolution_convert_fusion = bf16[3072,768]{1,0:T(8,128)(2,1)} fusion(bf16[512,3072]{1,0:T(8,128)(2,1)} %all-gather.5.cloned.1.call-done, bf16[512,384]{1,0:T(8,128)(2,1)S(1)} %bitcast.54, bf16[512,384]{1,0:T(8,128)(2,1)S(1)} %bitcast.55), kind=kOutput, calls=%fused_computation | convolution fusion | flops 2419851264 | bytes 8650752 | tf_op jit(solution)/shard_map/dot_general | solution.py:45
  203.1 136.8 %reduce-scatter.2.cloned.1.call-done = f32[32,3072]{1,0:T(8,128)} async-done(((f32[512,3072]{1,0:T(8,128)}), f32[32,3072]{1,0:T(8,128)}) %reduce-scatter.2.cloned.1.call-update) | async-done | bytes 393232 | tf_op jit(solution)/shard_map/reduce_scatter | solution.py:63
  339.9 1.4 fusion
  341.3 2.8 collective-permute-start
  344.1 5.0 %slice_bitcast_fusion = (bf16[1,3072,384]{2,1,0:T(8,128)(2,1)}, bf16[1,3072,384]{2,1,0:T(8,128)(2,1)}) fusion(bf16[3072,768]{1,0:T(8,128)(2,1)} %convolution_convert_fusion), kind=kLoop, calls=%fused_computation.6 | loop fusion | bytes 9437184 | tf_op jit(solution)/shard_map/broadcast_in_dim | solution.py:75
  349.2 12.8 %collective-permute-done = bf16[1,128,3072]{2,1,0:T(8,128)(2,1)S(1)} collective-permute-done((bf16[1,128,3072]{2,1,0:T(8,128)(2,1)S(1)}, bf16[1,128,3072]{2,1,0:T(8,128)(2,1)S(1)}, u32[]{:S(2)}, u32[]{:S(2)}) %collective-permute-start) | collective-permute-done | bytes 786464 | tf_op jit(solution)/shard_map/ppermute | solution.py:12
  362.0 0.9 copy.24
  (24 shorter events, 0.4 us)
Async XLA Ops:
  7.2 104.3 %copy-start = (bf16[1,3072,384]{2,1,0:T(8,128)(2,1)S(1)}, bf16[1,3072,384]{2,1,0:T(8,128)(2,1)}, u32[]{:S(2)}) copy-start(bf16[1,3072,384]{2,1,0:T(8,128)(2,1)} %param.19) | copy-start | bytes 7077892
  7.2 6.8 %copy-start.1 = (bf16[1,32,6144]{2,1,0:T(8,128)(2,1)S(1)}, bf16[1,32,6144]{2,1,0:T(8,128)(2,1)}, u32[]{:S(2)}) copy-start(bf16[1,32,6144]{2,1,0:T(8,128)(2,1)} %param.13) | copy-start | bytes 1179652
  7.2 98.8 %all-gather.3.cloned.1.call-start = ((), (), s32[]{:S(2)}) async-start(), calls=%async_computation.2 | async-start | bytes 3342336 | tf_op jit(solution)/shard_map/all_gather | solution.py:41
  10.7 185.6 %all-gather.5.cloned.1.call-start = ((), (), s32[]{:S(2)}) async-start(), calls=%async_computation.4 | async-start | bytes 3342336 | tf_op jit(solution)/shard_map/all_gather | solution.py:46
  13.9 326.0 %reduce-scatter.2.cloned.1.call-start = ((), (), s32[]{:S(2)}) async-start(), calls=%async_computation.3 | async-start | bytes 6684672 | tf_op jit(solution)/shard_map/reduce_scatter | solution.py:63
  111.5 9.1 %copy-start.2 = (bf16[512,384]{1,0:T(8,128)(2,1)S(1)}, bf16[512,384]{1,0:T(8,128)(2,1)}, u32[]{:S(2)}) copy-start(bf16[512,384]{1,0:T(8,128)(2,1)} %get-tuple-element.7) | copy-start | bytes 1179652
  127.9 68.4 %copy-start.3 = (bf16[1,512,384]{2,1,0:T(8,128)(2,1)S(1)}, bf16[1,512,384]{2,1,0:T(8,128)(2,1)}, u32[]{:S(2)}) copy-start(bf16[1,512,384]{2,1,0:T(8,128)(2,1)} %param.17) | copy-start | bytes 1179652
  127.9 68.4 %copy-start.4 = (bf16[1,512,384]{2,1,0:T(8,128)(2,1)S(1)}, bf16[1,512,384]{2,1,0:T(8,128)(2,1)}, u32[]{:S(2)}) copy-start(bf16[1,512,384]{2,1,0:T(8,128)(2,1)} %param.16) | copy-start | bytes 1179652
  341.3 20.7 %collective-permute-start = (bf16[1,128,3072]{2,1,0:T(8,128)(2,1)S(1)}, bf16[1,128,3072]{2,1,0:T(8,128)(2,1)S(1)}, u32[]{:S(2)}, u32[]{:S(2)}) collective-permute-start(bf16[1,128,3072]{2,1,0:T(8,128)(2,1)S(1)} %fusion), channel_id=1, source_target_pairs={{16,0},{32,16},{48,32},{64,48},{80,64},{96,80},{112,96},{128,112},... | collective-permute-start | bytes 2359304 | tf_op jit(solution)/shard_map/ppermute | solution.py:12
Sparse Core Ops, SparseCore 0:
  10.8 95.2 all-gather.2
  108.4 87.8 all-gather.4
  198.8 141.0 reduce-scatter.1
where the time goes:
time: 374 us; the launch traced here: 369 us
  waiting for transfers between devices  283 us (76%)
  matrix products  34.2 us (9%)
  blocking collectives  26.9 us (7%)
  between operations  13.9 us (4%)
  local copies, waits for them, and re-layouts  6.29 us (2%)
    reduce_scatter x1, waiting for transfers between devices, shards(): lax.psum_scatter(term + lax.dot_general(up_grad, up_w, feature_dims, pref...  137 us
    all_gather x1, waiting for transfers between devices, shards(): lax.all_gather(packed_old, ('expert', 'dp'), axis=0, tiled=True)  68.2 us
    all_gather x1, waiting for transfers between devices, shards(): piece = lax.all_gather(packed, ('expert', 'dp'), axis=0, tiled=True)  64.9 us
    all_to_all x1, blocking collectives, shards(): lax.all_to_all(hidden_now[0], ('expert', 'dp'), split_axis=1, concat_axis...  26.9 us
    ppermute x1, waiting for transfers between devices, from_behind(): return lax.ppermute(array, axis, pairs)  12.8 us
    dot_general x1, matrix products, shards(): lax.dot_general(gate_grad, gate_w, feature_dims, preferred_element_type=j...  9.09 us
  transfers between devices with their start and end apart: 4, of which 4 were waited for; matrix products, arithmetic and copies ran while one was open for 10% of the time, Pallas kernels for 0%

commit v1 on v0

v1 whole, which is shorter than its diff:
```python
import jax
import jax.numpy as jnp
from jax import lax
from jax.experimental import pallas as pl
from jax.experimental.pallas import tpu as pltpu
from jax.sharding import PartitionSpec as P

EXPERTS = 16
RING = 8
CAP = 32
TOK = 128
D = 3072
WIDTH = 384
BOTH = 2 * WIDTH
LANE = RING * CAP
PIECES = 2
PIECE = D // PIECES
CHUNKS = 4
CHUNK = D // CHUNKS
MESH = pl.DeviceIdType.MESH
F32 = jnp.float32
BF16 = jnp.bfloat16


def routing(ids, expert):
    hits = (ids == expert).astype(F32)
    routed = jnp.sum(hits, axis=0, keepdims=True)
    earlier = lax.broadcasted_iota(jnp.int32, (TOK, TOK), 0) < lax.broadcasted_iota(
        jnp.int32, (TOK, TOK), 1
    )
    counts = jnp.dot(
        jnp.broadcast_to(routed, (16, TOK)).astype(BF16),
        earlier.astype(F32).astype(BF16),
        preferred_element_type=F32,
    )
    slot = counts[0:1].astype(jnp.int32)
    places = lax.broadcasted_iota(jnp.int32, (CAP, TOK), 0)
    table = jnp.where((slot == places) & (routed == 1.0), 1.0, 0.0)
    return table, hits


def kernel(
    ids_now, gates_now, ids_old, x_now, hidden, x_old, gate_old, up_old, w_gate, w_up,
    out, dw_gate, dw_up,
    ids_now_v, gates_now_v, ids_old_v, x_now_v, x_old_v, hid, old, wts, rows_now, rows_old,
    grads, term, send_r, send_l, send_o, land_r, land_l, land_o, tab_out, tab_in,
    load_sem, now_ss, now_rs, old_ss, old_rs, sib_ss, sib_rs, hid_ss, hid_rs, w_ss, w_rs,
    tab_ss, tab_rs, red_ss, red_rs, own_ss, own_rs,
):
    sections = lax.axis_size("section")
    s = lax.axis_index("section")
    e = lax.axis_index("expert")
    z = lax.axis_index("dp") * 2 + e // 2
    k = lax.rem(e, 2)
    expert = lax.rem(s, EXPERTS)

    def chip(by):
        return lax.rem(z + (by + RING), RING)

    def device(by_section, by_z, by_core):
        there = chip(by_z)
        return (
            lax.rem(s + (by_section + sections), sections),
            lax.rem(there, 2) * 2 + lax.rem(k + by_core, 2),
            there // 2,
        )

    def group(there, core):
        return (lax.rem(there, 2) * 2 + core) * 4 + there // 2

    sent = []

    def send(src, dst, ss, rs, to):
        copy = pltpu.make_async_remote_copy(
            src_ref=src, dst_ref=dst, send_sem=ss, recv_sem=rs, device_id=to, device_id_type=MESH
        )
        copy.start()
        sent.append(copy)
        return copy

    barrier = pltpu.get_barrier_semaphore()
    partners = [device(0, by, 0) for by in range(1, RING)] + [device(0, 0, 1)]
    partners += [device(by, dz, 0) for by in (-1, 1) for dz in (-1, 0, 1)]
    for partner in partners:
        pl.semaphore_signal(barrier, inc=1, device_id=partner, device_id_type=MESH)

    loads = 0

    def load(src, dst):
        nonlocal loads
        copy = pltpu.make_async_copy(src, dst, load_sem.at[loads])
        copy.start()
        loads += 1
        return copy

    def columns(start, size, step=128):
        return pl.ds(pl.multiple_of(start, step), size)

    get_now = [load(ids_now, ids_now_v), load(gates_now, gates_now_v), load(x_now, x_now_v)]
    get_old = [load(ids_old, ids_old_v), load(x_old, x_old_v)]
    mine = pl.ds(pl.multiple_of(z * CAP, CAP), CAP)
    gate_place, up_place = columns(k * WIDTH, WIDTH), columns(BOTH + k * WIDTH, WIDTH)
    get_weights = [load(w_gate, wts.at[:, gate_place]), load(w_up, wts.at[:, up_place])]
    get_hidden = [
        load(
            hidden.at[:, columns(group(z, core) * WIDTH, WIDTH)],
            hid.at[mine, core * WIDTH : (core + 1) * WIDTH],
        )
        for core in range(2)
    ]
    get_stored = [load(gate_old, old.at[:, 0:WIDTH]), load(up_old, old.at[:, WIDTH:BOTH])]

    for copy in get_now:
        copy.wait()
    table, hits = routing(ids_now_v[...], expert)
    rows_now[mine, :] = jnp.dot(
        table.astype(BF16), x_now_v[...], preferred_element_type=F32
    ).astype(BF16)
    weight = jnp.sum(gates_now_v[...] * hits, axis=0, keepdims=True)
    coef = jnp.sum(table * weight, axis=1, keepdims=True)
    tab_out[:, 0:TOK] = table
    tab_out[:, TOK : 2 * TOK] = jnp.broadcast_to(coef, (CAP, TOK))

    pl.semaphore_wait(barrier, len(partners))

    def gather_hop(buf, place, ss, rs, hop, waits):
        copies = {}
        for piece in range(PIECES):
            for way, by in enumerate((1, -1)):
                if hop == 3 and (piece < PIECES // 2) != (way == 0):
                    continue
                if waits is not None:
                    waits[way, piece].wait_recv()
                block = buf.at[place(chip(-hop * by)), piece * PIECE : (piece + 1) * PIECE]
                at = (way * 4 + hop) * PIECES + piece
                copies[way, piece] = send(block, block, ss.at[at], rs.at[at], device(0, by, 0))
        return copies

    def now_place(there):
        return pl.ds(pl.multiple_of(there * CAP, CAP), CAP)

    def old_place(there):
        return pl.ds(pl.multiple_of(group(there, k) * CAP, CAP), CAP)

    siblings = []

    def share(by, first=0, last=D):
        block = rows_old.at[old_place(chip(by)), first:last]
        at = len(siblings)
        siblings.append(send(block, block, sib_ss.at[at], sib_rs.at[at], device(0, 0, 1)))

    now_0 = gather_hop(rows_now, now_place, now_ss, now_rs, 0, None)
    hidden_sent = []
    for by in range(1, RING):
        there = chip(by)
        for core in range(2):
            at = (by - 1) * 2 + core
            hidden_sent.append(
                send(
                    hidden.at[:, columns(group(there, core) * WIDTH, WIDTH)],
                    hid.at[mine, core * WIDTH : (core + 1) * WIDTH],
                    hid_ss.at[at],
                    hid_rs.at[at],
                    device(0, by, 0),
                )
            )
    weights_sent = [
        send(w_gate, wts.at[:, gate_place], w_ss.at[0], w_rs.at[0], device(0, 0, 1)),
        send(w_up, wts.at[:, up_place], w_ss.at[1], w_rs.at[1], device(0, 0, 1)),
    ]
    table_sent = send(tab_out, tab_in, tab_ss.at[0], tab_rs.at[0], device(-1, 0, 0))

    for copy in get_old:
        copy.wait()
    old_table, _ = routing(ids_old_v[...], expert)
    rows_old[old_place(z), :] = jnp.dot(
        old_table.astype(BF16), x_old_v[...], preferred_element_type=F32
    ).astype(BF16)

    now_1 = gather_hop(rows_now, now_place, now_ss, now_rs, 1, now_0)
    old_0 = gather_hop(rows_old, old_place, old_ss, old_rs, 0, None)
    share(0)
    now_2 = gather_hop(rows_now, now_place, now_ss, now_rs, 2, now_1)
    now_3 = gather_hop(rows_now, now_place, now_ss, now_rs, 3, now_2)
    old_1 = gather_hop(rows_old, old_place, old_ss, old_rs, 1, old_0)
    share(-1)
    share(1)

    for copy in get_weights + get_hidden + get_stored:
        copy.wait()
    for copy in hidden_sent + weights_sent:
        copy.wait_recv()
    for way in range(2):
        for piece in range(PIECES):
            if (way, piece) not in now_3:
                now_2[way, piece].wait_recv()
    for copy in now_3.values():
        copy.wait_recv()

    def gate_step(j):
        lanes = slice(j * 256, (j + 1) * 256)
        up_lanes = slice(BOTH + j * 256, BOTH + (j + 1) * 256)
        gate = jnp.dot(rows_now[...], wts[:, lanes], preferred_element_type=F32)
        up = jnp.dot(rows_now[...], wts[:, up_lanes], preferred_element_type=F32)
        incoming = hid[:, lanes].astype(F32)
        sig = 1.0 / (1.0 + jnp.exp(-gate))
        act = gate * sig
        slope = sig * (1.0 + gate * (1.0 - sig))
        grads[:, lanes] = (incoming * up * slope).astype(BF16)
        grads[:, up_lanes] = (incoming * act).astype(BF16)

    gate_step(0)
    gate_step(1)
    old_2 = gather_hop(rows_old, old_place, old_ss, old_rs, 2, old_1)
    share(-2)
    share(2)
    gate_step(2)

    def lanes_of(c):
        return slice(c * CHUNK, (c + 1) * CHUNK)

    moving = {}

    def push(c, way, hop):
        by = 1 - 2 * way
        lanes = lanes_of(c)
        value = term[now_place(chip((4 - hop) * by)), lanes]
        if (c, way, hop - 1) in moving:
            moving[c, way, hop - 1].wait_recv()
            value = value + (land_r, land_l)[way][hop - 1, :, lanes].astype(F32)
        src = (send_r, send_l)[way].at[hop, :, lanes]
        src[...] = value.astype(BF16)
        at = (way * 4 + hop) * CHUNKS + c
        moving[c, way, hop] = send(
            src,
            (land_r, land_l)[way].at[hop, :, lanes],
            red_ss.at[at],
            red_rs.at[at],
            device(-1 if hop == 3 else 0, by, 0),
        )

    order = (0, 2, 1, 3)
    own = {}

    def start_chunk(c):
        lanes = lanes_of(c)
        term[:, lanes] = lax.dot_general(
            grads[...], wts[lanes, :], (((1,), (1,)), ((), ())), preferred_element_type=F32
        )
        long = 0 if c < CHUNKS // 2 else 1
        push(c, long, 0)
        push(c, 1 - long, 1)
        send_o[:, lanes] = term[mine, lanes].astype(BF16)
        own[c] = send(
            send_o.at[:, lanes], land_o.at[:, lanes], own_ss.at[c], own_rs.at[c], device(-1, 0, 0)
        )

    start_chunk(order[0])
    start_chunk(order[1])
    old_3 = gather_hop(rows_old, old_place, old_ss, old_rs, 3, old_2)
    for way in range(2):
        for piece in range(PIECES):
            if (way, piece) not in old_3:
                old_2[way, piece].wait_recv()
    share(-3)
    share(3)
    start_chunk(order[2])
    start_chunk(order[3])

    def dw_step(i):
        rows = slice(i * 256, (i + 1) * 256)
        value = lax.dot_general(
            rows_old[:, rows], old[...], (((0,), (0,)), ((), ())), preferred_element_type=F32
        ).astype(BF16)
        dw_gate[rows, :] = value[:, 0:WIDTH]
        dw_up[rows, :] = value[:, WIDTH:BOTH]

    for turn in (1, 2, 3):
        for i, c in enumerate(order):
            long = 0 if c < CHUNKS // 2 else 1
            push(c, long, turn)
            if turn < 3:
                push(c, 1 - long, turn + 1)
            if turn == 1 and i == 0:
                for copy in old_3.values():
                    copy.wait_recv()
                share(4, 0, PIECE)
                share(4, PIECE, D)
                for copy in siblings:
                    copy.wait_recv()
            dw_step((turn - 1) * 4 + i)

    table_sent.wait_recv()
    back = tab_in[:, 0:TOK].astype(BF16)
    scale = tab_in[:, TOK : TOK + 1]
    last = s == sections - 1
    for c in order:
        lanes = lanes_of(c)
        own[c].wait_recv()
        moving[c, 0, 3].wait_recv()
        moving[c, 1, 3].wait_recv()
        total = (
            land_o[:, lanes].astype(F32)
            + land_r[3, :, lanes].astype(F32)
            + land_l[3, :, lanes].astype(F32)
        )
        spread = lax.dot_general(
            back, (scale * total).astype(BF16), (((0,), (0,)), ((), ())), preferred_element_type=F32
        )
        out[:, lanes] = jnp.where(last, 0.0, spread).astype(BF16)
    for copy in sent:
        copy.wait_send()


def shards(
    x_now, ids_now, gates_now, hidden_now, x_old, ids_old, gate_grad_old, up_grad_old, w_gate, w_up
):
    anywhere = pl.BlockSpec(memory_space=pl.ANY)
    dma = pltpu.SemaphoreType.DMA
    out, dw_gate, dw_up = pl.pallas_call(
        kernel,
        out_shape=(
            pltpu.VMEM((TOK, D), BF16),
            pltpu.VMEM((D, WIDTH), BF16),
            pltpu.VMEM((D, WIDTH), BF16),
        ),
        in_specs=[anywhere] * 10,
        out_specs=[pl.BlockSpec(memory_space=pltpu.VMEM)] * 3,
        scratch_shapes=[
            pltpu.VMEM((4, TOK), jnp.int32),
            pltpu.VMEM((4, TOK), F32),
            pltpu.VMEM((4, TOK), jnp.int32),
            pltpu.VMEM((TOK, D), BF16),
            pltpu.VMEM((TOK, D), BF16),
            pltpu.VMEM((LANE, BOTH), BF16),
            pltpu.VMEM((2 * LANE, BOTH), BF16),
            pltpu.VMEM((D, 2 * BOTH), BF16),
            pltpu.VMEM((LANE, D), BF16),
            pltpu.VMEM((2 * LANE, D), BF16),
            pltpu.VMEM((LANE, 2 * BOTH), BF16),
            pltpu.VMEM((LANE, D), F32),
            pltpu.VMEM((4, CAP, D), BF16),
            pltpu.VMEM((4, CAP, D), BF16),
            pltpu.VMEM((CAP, D), BF16),
            pltpu.VMEM((4, CAP, D), BF16),
            pltpu.VMEM((4, CAP, D), BF16),
            pltpu.VMEM((CAP, D), BF16),
            pltpu.VMEM((CAP, 2 * TOK), F32),
            pltpu.VMEM((CAP, 2 * TOK), F32),
            dma((11,)),
            dma((8 * PIECES,)),
            dma((8 * PIECES,)),
            dma((8 * PIECES,)),
            dma((8 * PIECES,)),
            dma((9,)),
            dma((9,)),
            dma((14,)),
            dma((14,)),
            dma((2,)),
            dma((2,)),
            dma((1,)),
            dma((1,)),
            dma((8 * CHUNKS,)),
            dma((8 * CHUNKS,)),
            dma((CHUNKS,)),
            dma((CHUNKS,)),
        ],
        compiler_params=pltpu.CompilerParams(
            collective_id=0, has_side_effects=True, vmem_limit_bytes=48 << 20
        ),
        cost_estimate=pl.CostEstimate(
            flops=3 * 2 * 512 * D * BOTH, bytes_accessed=16 << 20, transcendentals=512 * WIDTH
        ),
    )(
        ids_now[0].T, gates_now[0].T, ids_old[0].T, x_now[0], hidden_now[0], x_old[0],
        gate_grad_old[0], up_grad_old[0], w_gate[0], w_up[0],
    )
    return out[None], dw_gate[None], dw_up[None]


def solution(mesh):
    in_specs = (
        P("section", ("expert", "dp"), None),
        P("section", ("expert", "dp"), None),
        P("section", ("expert", "dp"), None),
        P("section", ("expert", "dp"), None),
        P("section", ("expert", "dp"), None),
        P("section", ("expert", "dp"), None),
        P("section", None, ("expert", "dp")),
        P("section", None, ("expert", "dp")),
        P("section", None, ("expert", "dp")),
        P("section", None, ("expert", "dp")),
    )
    out_specs = (
        P("section", ("expert", "dp"), None),
        P("section", None, ("expert", "dp")),
        P("section", None, ("expert", "dp")),
    )
    return jax.shard_map(shards, mesh=mesh, in_specs=in_specs, out_specs=out_specs, check_vma=False)
```

time: 374 us -> 79.8 us (0.21); the launches traced: 369 us -> 79.3 us
  waiting for transfers between devices: 283 us -> 0 us
  Pallas kernels: 0 us -> 71.9 us
  matrix products: 34.2 us -> 0 us
  blocking collectives: 26.9 us -> 0 us
  between operations: 13.9 us -> 0.65 us
    reduce_scatter x1 -> x0, waiting for transfers between devices: 137 us -> none  [shards(): lax.psum_scatter(term + lax.dot_general(up_grad, up_w, feature_dims, pref...]
    all_gather x2 -> x0, waiting for transfers between devices: 133 us -> none  [the longest x1 68.2 us: shards(): lax.all_gather(packed_old, ('expert', 'dp'), axis=0, tiled=True)]
    pallas_call x0 -> x1, Pallas kernels: none -> 71.9 us  [shards(): pl.pallas_call(kernel, out_shape=(pltpu.VMEM((TOK, D), BF16), pltpu.VMEM(...]
    dot_general x7 -> x0, matrix products: 34.2 us -> none  [the longest x1 9.09 us: shards(): lax.dot_general(gate_grad, gate_w, feature_dims, preferred_element_type=j...]
    all_to_all x1 -> x0, blocking collectives: 26.9 us -> none  [shards(): lax.all_to_all(hidden_now[0], ('expert', 'dp'), split_axis=1, concat_axis...]
    ppermute x1 -> x0, waiting for transfers between devices: 12.8 us -> none  [from_behind(): return lax.ppermute(array, axis, pairs)]
    unnamed x12 -> x11, local copies, waits for them, and re-layouts: 0.95 us -> 6.72 us
    broadcast_in_dim x1 -> x0, local copies, waits for them, and re-layouts: 5.03 us -> none  [shards(): dw_up = weight_sum[:, width:].astype(jnp.bfloat16)[None]]
  transfers between devices with their start and end apart: 4 -> 0, of which waited for: 4 -> 0; matrix products, arithmetic and copies ran while one was open for 10% -> 0% of each run, Pallas kernels for 0% -> 0%
where the time goes in v1:
time: 79.8 us; the launch traced here: 79.3 us
  Pallas kernels  71.9 us (90%)
  local copies, waits for them, and re-layouts  6.72 us (8%)
    pallas_call x1, Pallas kernels, shards(): pl.pallas_call(kernel, out_shape=(pltpu.VMEM((TOK, D), BF16), pltpu.VMEM(...  71.9 us
    unnamed x11, local copies, waits for them, and re-layouts  6.72 us

profile of v1, /device:TPU:30, one launch (start us, length us, event | category | flops | bytes accessed | tf_op | source)
XLA Modules:
  0.0 79.3 jit_solution(6580088618147635969)
XLA Ops:
  0.6 0.0 copy-start
  0.6 1.0 %copy-done = bf16[1,32,6144]{2,1,0:T(8,128)(2,1)S(1)} copy-done((bf16[1,32,6144]{2,1,0:T(8,128)(2,1)S(1)}, bf16[1,32,6144]{2,1,0:T(8,128)(2,1)}, u32[]{:S(2)}) %copy-start) | copy-done | bytes 393240
  1.6 0.0 copy-start.1
  1.6 0.7 copy-done.1
  2.3 0.0 copy-start.2
  2.3 0.7 copy-done.2
  3.0 0.0 copy-start.3
  3.0 0.7 copy-done.3
  3.7 71.9 %shard_map.121 = (bf16[128,3072]{1,0:T(8,128)(2,1)S(1)}, bf16[3072,384]{1,0:T(8,128)(2,1)S(1)}, bf16[3072,384]{1,0:T(8,128)(2,1)S(1)}) custom-call(s32[4,128]{1,0:T(4,128)S(1)} %bitcast.23, f32[4,128]{1,0:T(4,128)S(1)} %bitcast.24, s32[4,128]{1,0:T(4,128)S(1)} %bitcast.25, bf16[128,3072]{1,0:T(8,128)(2,1)} %bitcast.28, bf16[32,6144]{1,0:T(8,128)(2,1)S(1)} %bitcast.22, ...), custom_call_target="tpu_custom_call" | custom-call | flops 7247757312 | bytes 16777216 | tf_op jit(solution)/shard_map/pallas_call | solution.py:320
  75.6 0.9 %copy.16 = bf16[1,128,3072]{2,1,0:T(8,128)(2,1)} copy(bf16[1,128,3072]{2,1,0:T(8,128)(2,1)S(1)} %bitcast.21) | data formatting | bytes 1572864
  76.4 1.4 %copy.17 = bf16[1,3072,384]{2,1,0:T(8,128)(2,1)} copy(bf16[1,3072,384]{2,1,0:T(8,128)(2,1)S(1)} %bitcast.20) | data formatting | bytes 4718592
  77.8 1.4 %copy.18 = bf16[1,3072,384]{2,1,0:T(8,128)(2,1)} copy(bf16[1,3072,384]{2,1,0:T(8,128)(2,1)S(1)} %bitcast.19) | data formatting | bytes 4718592
Async XLA Ops:
  0.6 1.0 %copy-start = (bf16[1,32,6144]{2,1,0:T(8,128)(2,1)S(1)}, bf16[1,32,6144]{2,1,0:T(8,128)(2,1)}, u32[]{:S(2)}) copy-start(bf16[1,32,6144]{2,1,0:T(8,128)(2,1)} %param.13) | copy-start | bytes 1179652
  1.6 0.7 copy-start.1
  2.3 0.7 copy-start.2
  3.0 0.7 copy-start.3

commit v2 on v1

v2 whole, which is shorter than its diff:
```python
import jax
import jax.numpy as jnp
from jax import lax
from jax.experimental import pallas as pl
from jax.experimental.pallas import tpu as pltpu
from jax.sharding import PartitionSpec as P

EXPERTS = 16
RING = 8
CAP = 32
TOK = 128
D = 3072
WIDTH = 384
BOTH = 2 * WIDTH
LANE = RING * CAP
PIECES = 2
PIECE = D // PIECES
CHUNKS = 4
CHUNK = D // CHUNKS
ORDER = (0, -1, 1, -2, 2, -3, 3, 4)
NEAR, FAR = slice(0, 5 * CAP), slice(5 * CAP, LANE)
MESH = pl.DeviceIdType.MESH
F32 = jnp.float32
BF16 = jnp.bfloat16


def routing(ids, expert):
    hits = (ids == expert).astype(F32)
    routed = jnp.sum(hits, axis=0, keepdims=True)
    earlier = lax.broadcasted_iota(jnp.int32, (TOK, TOK), 0) < lax.broadcasted_iota(
        jnp.int32, (TOK, TOK), 1
    )
    counts = jnp.dot(
        jnp.broadcast_to(routed, (16, TOK)).astype(BF16),
        earlier.astype(F32).astype(BF16),
        preferred_element_type=F32,
    )
    slot = counts[0:1].astype(jnp.int32)
    places = lax.broadcasted_iota(jnp.int32, (CAP, TOK), 0)
    table = jnp.where((slot == places) & (routed == 1.0), 1.0, 0.0)
    return table, hits


def kernel(
    ids_now, gates_now, ids_old, x_now, hidden, x_old, gate_old, up_old, w_gate, w_up,
    packed_grad, tab_in, dw_gate, dw_up,
    ids_now_v, gates_now_v, ids_old_v, x_now_v, x_old_v, hid, old, wts, rows_now, rows_old,
    grads, term, send_r, send_l, send_o, land_r, land_l, land_o, tab_out,
    load_sem, now_ss, now_rs, old_ss, old_rs, sib_ss, sib_rs, hid_ss, hid_rs, w_ss, w_rs,
    tab_ss, tab_rs, red_ss, red_rs, own_ss, own_rs,
):
    sections = lax.axis_size("section")
    s = lax.axis_index("section")
    e = lax.axis_index("expert")
    z = lax.axis_index("dp") * 2 + e // 2
    k = lax.rem(e, 2)
    expert = lax.rem(s, EXPERTS)

    def chip(by):
        return lax.rem(z + (by + RING), RING)

    def device(by_section, by_z, by_core):
        there = chip(by_z)
        return (
            lax.rem(s + (by_section + sections), sections),
            lax.rem(there, 2) * 2 + lax.rem(k + by_core, 2),
            there // 2,
        )

    def group(there, core):
        return (lax.rem(there, 2) * 2 + core) * 4 + there // 2

    sent = []

    def send(src, dst, ss, rs, to):
        copy = pltpu.make_async_remote_copy(
            src_ref=src, dst_ref=dst, send_sem=ss, recv_sem=rs, device_id=to, device_id_type=MESH
        )
        copy.start()
        sent.append(copy)
        return copy

    barrier = pltpu.get_barrier_semaphore()
    partners = [device(0, 1, 0), device(0, -1, 0), device(0, 0, 1)]
    partners += [device(-1, 0, 0), device(1, 0, 0)]
    for partner in partners:
        pl.semaphore_signal(barrier, inc=1, device_id=partner, device_id_type=MESH)

    loads = 0

    def load(src, dst):
        nonlocal loads
        copy = pltpu.make_async_copy(src, dst, load_sem.at[loads])
        copy.start()
        loads += 1
        return copy

    def columns(start, size, step=128):
        return pl.ds(pl.multiple_of(start, step), size)

    def place(by):
        at = ORDER.index((by + 3) % RING - 3) * CAP
        return slice(at, at + CAP)

    get_now = [load(ids_now, ids_now_v), load(gates_now, gates_now_v), load(x_now, x_now_v)]
    for copy in get_now:
        copy.wait()
    get_old = [load(ids_old, ids_old_v), load(x_old, x_old_v)]
    gate_place, up_place = columns(k * WIDTH, WIDTH), columns(BOTH + k * WIDTH, WIDTH)
    get_weights = [load(w_gate, wts.at[:, gate_place]), load(w_up, wts.at[:, up_place])]
    get_hidden = [
        load(
            hidden.at[:, columns(group(z, core) * WIDTH, WIDTH)],
            hid.at[place(0), core * WIDTH : (core + 1) * WIDTH],
        )
        for core in range(2)
    ]
    get_stored = [load(gate_old, old.at[:, 0:WIDTH]), load(up_old, old.at[:, WIDTH:BOTH])]

    table, hits = routing(ids_now_v[...], expert)
    rows_now[place(0), :] = jnp.dot(
        table.astype(BF16), x_now_v[...], preferred_element_type=F32
    ).astype(BF16)
    weight = jnp.sum(gates_now_v[...] * hits, axis=0, keepdims=True)
    coef = jnp.sum(table * weight, axis=1, keepdims=True)
    tab_out[:, 0:TOK] = table
    tab_out[:, TOK : 2 * TOK] = jnp.broadcast_to(coef, (CAP, TOK))

    pl.semaphore_wait(barrier, len(partners))

    def gather_hop(buf, src, dst, ss, rs, hop, waits):
        copies = {}
        for piece in range(PIECES):
            for way, by in enumerate((1, -1)):
                if hop == 3 and (piece < PIECES // 2) != (way == 0):
                    continue
                if waits is not None:
                    waits[way, piece].wait_recv()
                lanes = slice(piece * PIECE, (piece + 1) * PIECE)
                at = (way * 4 + hop) * PIECES + piece
                copies[way, piece] = send(
                    buf.at[src(hop, by), lanes],
                    buf.at[dst(hop, by), lanes],
                    ss.at[at],
                    rs.at[at],
                    device(0, by, 0),
                )
        return copies

    def now_hop(hop, waits):
        def src(hop, by):
            return place(-hop * by)

        def dst(hop, by):
            return place(-(hop + 1) * by)

        return gather_hop(rows_now, src, dst, now_ss, now_rs, hop, waits)

    def old_place(there):
        return pl.ds(pl.multiple_of(group(there, k) * CAP, CAP), CAP)

    def old_hop(hop, waits):
        def both(hop, by):
            return old_place(chip(-hop * by))

        return gather_hop(rows_old, both, both, old_ss, old_rs, hop, waits)

    def arrive(before, after):
        for key, copy in before.items():
            if key not in after:
                copy.wait_recv()

    siblings = []

    def share(by, first=0, last=D):
        block = rows_old.at[old_place(chip(by)), first:last]
        at = len(siblings)
        siblings.append(send(block, block, sib_ss.at[at], sib_rs.at[at], device(0, 0, 1)))

    hidden_sent = {}

    def send_hidden(by):
        there = chip(by)
        for core in range(2):
            at = (by % RING - 1) * 2 + core
            hidden_sent[by, core] = send(
                hidden.at[:, columns(group(there, core) * WIDTH, WIDTH)],
                hid.at[place(-by), core * WIDTH : (core + 1) * WIDTH],
                hid_ss.at[at],
                hid_rs.at[at],
                device(0, by, 0),
            )

    now_0 = now_hop(0, None)
    weights_sent = [
        send(w_gate, wts.at[:, gate_place], w_ss.at[0], w_rs.at[0], device(0, 0, 1)),
        send(w_up, wts.at[:, up_place], w_ss.at[1], w_rs.at[1], device(0, 0, 1)),
    ]
    for by in (1, -1):
        send_hidden(by)
    table_sent = send(tab_out, tab_in, tab_ss.at[0], tab_rs.at[0], device(-1, 0, 0))

    for copy in get_old:
        copy.wait()
    old_table, _ = routing(ids_old_v[...], expert)
    rows_old[old_place(z), :] = jnp.dot(
        old_table.astype(BF16), x_old_v[...], preferred_element_type=F32
    ).astype(BF16)

    old_0 = old_hop(0, None)
    share(0)
    now_1 = now_hop(1, now_0)
    for by in (2, -2):
        send_hidden(by)
    now_2 = now_hop(2, now_1)
    for by in (3, -3):
        send_hidden(by)

    for copy in get_weights + get_hidden + get_stored:
        copy.wait()
    for copy in weights_sent:
        copy.wait_recv()

    def gate_step(rows, j):
        lanes = slice(j * 256, (j + 1) * 256)
        up_lanes = slice(BOTH + j * 256, BOTH + (j + 1) * 256)
        gate = jnp.dot(rows_now[rows, :], wts[:, lanes], preferred_element_type=F32)
        up = jnp.dot(rows_now[rows, :], wts[:, up_lanes], preferred_element_type=F32)
        incoming = hid[rows, lanes].astype(F32)
        sig = 1.0 / (1.0 + jnp.exp(-gate))
        act = gate * sig
        slope = sig * (1.0 + gate * (1.0 - sig))
        grads[rows, lanes] = (incoming * up * slope).astype(BF16)
        grads[rows, up_lanes] = (incoming * act).astype(BF16)

    def lanes_of(c):
        return slice(c * CHUNK, (c + 1) * CHUNK)

    def term_step(rows, c):
        term[rows, lanes_of(c)] = lax.dot_general(
            grads[rows, :], wts[lanes_of(c), :], (((1,), (1,)), ((), ())), preferred_element_type=F32
        )

    for by in (1, -1, 2, -2):
        for core in range(2):
            hidden_sent[by, core].wait_recv()
    for j in range(3):
        gate_step(NEAR, j)
    now_3 = now_hop(3, now_2)
    send_hidden(4)
    for c in range(CHUNKS):
        term_step(NEAR, c)
    old_1 = old_hop(1, old_0)
    share(-1)
    share(1)

    moving = {}

    def push(c, way, hop):
        by = 1 - 2 * way
        lanes = lanes_of(c)
        value = term[place((4 - hop) * by), lanes]
        if (c, way, hop - 1) in moving:
            moving[c, way, hop - 1].wait_recv()
            value = value + (land_r, land_l)[way][hop - 1, :, lanes].astype(F32)
        src = (send_r, send_l)[way].at[hop, :, lanes]
        src[...] = value.astype(BF16)
        at = (way * 4 + hop) * CHUNKS + c
        moving[c, way, hop] = send(
            src,
            (land_r, land_l)[way].at[hop, :, lanes],
            red_ss.at[at],
            red_rs.at[at],
            device(-1 if hop == 3 else 0, by, 0),
        )

    order = (0, 2, 1, 3)

    def long_way(c):
        return 0 if c < CHUNKS // 2 else 1

    arrive(now_2, now_3)
    for copy in now_3.values():
        copy.wait_recv()
    for by in (3, -3, 4):
        for core in range(2):
            hidden_sent[by, core].wait_recv()
    for j in range(3):
        gate_step(FAR, j)
    for c in order:
        term_step(FAR, c)
        push(c, long_way(c), 0)
        push(c, 1 - long_way(c), 1)
    old_2 = old_hop(2, old_1)
    share(-2)
    share(2)
    send_o[...] = term[place(0), :].astype(BF16)
    own = send(send_o, land_o, own_ss.at[0], own_rs.at[0], device(-1, 0, 0))

    def dw_step(i):
        rows = slice(i * 256, (i + 1) * 256)
        value = lax.dot_general(
            rows_old[:, rows], old[...], (((0,), (0,)), ((), ())), preferred_element_type=F32
        ).astype(BF16)
        dw_gate[rows, :] = value[:, 0:WIDTH]
        dw_up[rows, :] = value[:, WIDTH:BOTH]

    for c in order:
        push(c, long_way(c), 1)
    for c in order:
        push(c, 1 - long_way(c), 2)
    old_3 = old_hop(3, old_2)
    arrive(old_2, old_3)
    share(-3)
    share(3)
    for c in order:
        push(c, long_way(c), 2)
    for c in order:
        push(c, 1 - long_way(c), 3)
    for copy in old_3.values():
        copy.wait_recv()
    share(4, 0, D // 2)
    share(4, D // 2, D)
    for c in order:
        push(c, long_way(c), 3)
    for copy in siblings:
        copy.wait_recv()
    for i in range(12):
        dw_step(i)

    table_sent.wait_recv()
    own.wait_recv()
    scale = tab_in[:, TOK : TOK + 1]
    for c in order:
        lanes = lanes_of(c)
        moving[c, 0, 3].wait_recv()
        moving[c, 1, 3].wait_recv()
        total = (
            land_o[:, lanes].astype(F32)
            + land_r[3, :, lanes].astype(F32)
            + land_l[3, :, lanes].astype(F32)
        )
        packed_grad[:, lanes] = (scale * total).astype(BF16)
    for copy in sent:
        copy.wait_send()


def finish(packed_grad, tab, dw_gate, dw_up, out, out_gate, out_up, spread, sem):
    copies = []
    for src, dst in ((dw_gate, out_gate), (dw_up, out_up)):
        for part in range(2):
            rows = slice(part * (D // 2), (part + 1) * (D // 2))
            copies.append(pltpu.make_async_copy(src.at[rows], dst.at[rows], sem.at[len(copies)]))
            copies[-1].start()
    last = lax.axis_index("section") == lax.axis_size("section") - 1
    back = tab[:, 0:TOK].astype(BF16)
    for c in range(2):
        lanes = slice(c * (D // 2), (c + 1) * (D // 2))
        value = lax.dot_general(
            back, packed_grad[:, lanes], (((0,), (0,)), ((), ())), preferred_element_type=F32
        )
        spread[:, lanes] = jnp.where(last, 0.0, value).astype(BF16)
        copies.append(pltpu.make_async_copy(spread.at[:, lanes], out.at[:, lanes], sem.at[4 + c]))
        copies[-1].start()
    for copy in copies:
        copy.wait()


def shards(
    x_now, ids_now, gates_now, hidden_now, x_old, ids_old, gate_grad_old, up_grad_old, w_gate, w_up
):
    anywhere = pl.BlockSpec(memory_space=pl.ANY)
    dma = pltpu.SemaphoreType.DMA
    inputs = [
        ids_now[0].T, gates_now[0].T, ids_old[0].T, x_now[0], hidden_now[0], x_old[0],
        gate_grad_old[0], up_grad_old[0], w_gate[0], w_up[0],
    ]
    inputs = [pltpu.with_memory_space_constraint(array, pltpu.HBM) for array in inputs]
    packed_grad, tab, dw_gate, dw_up = pl.pallas_call(
        kernel,
        out_shape=(
            pltpu.VMEM((CAP, D), BF16),
            pltpu.VMEM((CAP, 2 * TOK), F32),
            pltpu.VMEM((D, WIDTH), BF16),
            pltpu.VMEM((D, WIDTH), BF16),
        ),
        in_specs=[anywhere] * 10,
        out_specs=[pl.BlockSpec(memory_space=pltpu.VMEM)] * 4,
        scratch_shapes=[
            pltpu.VMEM((4, TOK), jnp.int32),
            pltpu.VMEM((4, TOK), F32),
            pltpu.VMEM((4, TOK), jnp.int32),
            pltpu.VMEM((TOK, D), BF16),
            pltpu.VMEM((TOK, D), BF16),
            pltpu.VMEM((LANE, BOTH), BF16),
            pltpu.VMEM((2 * LANE, BOTH), BF16),
            pltpu.VMEM((D, 2 * BOTH), BF16),
            pltpu.VMEM((LANE, D), BF16),
            pltpu.VMEM((2 * LANE, D), BF16),
            pltpu.VMEM((LANE, 2 * BOTH), BF16),
            pltpu.VMEM((LANE, D), F32),
            pltpu.VMEM((4, CAP, D), BF16),
            pltpu.VMEM((4, CAP, D), BF16),
            pltpu.VMEM((CAP, D), BF16),
            pltpu.VMEM((4, CAP, D), BF16),
            pltpu.VMEM((4, CAP, D), BF16),
            pltpu.VMEM((CAP, D), BF16),
            pltpu.VMEM((CAP, 2 * TOK), F32),
            dma((11,)),
            dma((8 * PIECES,)),
            dma((8 * PIECES,)),
            dma((8 * PIECES,)),
            dma((8 * PIECES,)),
            dma((9,)),
            dma((9,)),
            dma((14,)),
            dma((14,)),
            dma((2,)),
            dma((2,)),
            dma((1,)),
            dma((1,)),
            dma((8 * CHUNKS,)),
            dma((8 * CHUNKS,)),
            dma((1,)),
            dma((1,)),
        ],
        compiler_params=pltpu.CompilerParams(
            collective_id=0, has_side_effects=True, vmem_limit_bytes=48 << 20
        ),
        cost_estimate=pl.CostEstimate(
            flops=3 * 2 * 512 * D * BOTH, bytes_accessed=16 << 20, transcendentals=512 * WIDTH
        ),
    )(*inputs)
    out, dw_gate, dw_up = pl.pallas_call(
        finish,
        out_shape=(
            jax.ShapeDtypeStruct((TOK, D), BF16),
            jax.ShapeDtypeStruct((D, WIDTH), BF16),
            jax.ShapeDtypeStruct((D, WIDTH), BF16),
        ),
        in_specs=[pl.BlockSpec(memory_space=pltpu.VMEM)] * 4,
        out_specs=[pl.BlockSpec(memory_space=pltpu.HBM)] * 3,
        scratch_shapes=[pltpu.VMEM((TOK, D), BF16), dma((6,))],
        compiler_params=pltpu.CompilerParams(vmem_limit_bytes=16 << 20),
    )(packed_grad, tab, dw_gate, dw_up)
    return out[None], dw_gate[None], dw_up[None]


def solution(mesh):
    in_specs = (
        P("section", ("expert", "dp"), None),
        P("section", ("expert", "dp"), None),
        P("section", ("expert", "dp"), None),
        P("section", ("expert", "dp"), None),
        P("section", ("expert", "dp"), None),
        P("section", ("expert", "dp"), None),
        P("section", None, ("expert", "dp")),
        P("section", None, ("expert", "dp")),
        P("section", None, ("expert", "dp")),
        P("section", None, ("expert", "dp")),
    )
    out_specs = (
        P("section", ("expert", "dp"), None),
        P("section", None, ("expert", "dp")),
        P("section", None, ("expert", "dp")),
    )
    return jax.shard_map(shards, mesh=mesh, in_specs=in_specs, out_specs=out_specs, check_vma=False)
```

time: 79.8 us -> 71.9 us (0.901)
  local copies, waits for them, and re-layouts: 6.72 us -> 0 us
  Pallas kernels: 71.9 us -> 71.1 us
    unnamed x11 -> x0, local copies, waits for them, and re-layouts: 6.72 us -> none
    pallas_call x1 -> x2, Pallas kernels: 71.9 us -> 71.1 us  [the longest x1 68.6 us: shards(): pl.pallas_call(kernel, out_shape=(pltpu.VMEM((CAP, D), BF16), pltpu.VMEM(...]
where the time goes in v2:
time: 71.9 us; the launch traced here: 71.8 us
  Pallas kernels  71.1 us (99%)
    pallas_call x1, Pallas kernels, shards(): pl.pallas_call(kernel, out_shape=(pltpu.VMEM((CAP, D), BF16), pltpu.VMEM(...  68.6 us
    pallas_call x1, Pallas kernels, shards(): pl.pallas_call(finish, out_shape=(jax.ShapeDtypeStruct((TOK, D), BF16), j...  2.47 us

profile of v2, /device:TPU:30, one launch (start us, length us, event | category | flops | bytes accessed | tf_op | source)
XLA Modules:
  0.0 71.8 jit_solution(8978290190866223212)
XLA Ops:
  0.6 68.6 %shard_map.121 = (bf16[32,3072]{1,0:T(8,128)(2,1)S(1)}, f32[32,256]{1,0:T(8,128)S(1)}, bf16[3072,384]{1,0:T(8,128)(2,1)S(1)}, bf16[3072,384]{1,0:T(8,128)(2,1)S(1)}) custom-call(s32[4,128]{1,0:T(4,128)} %bitcast.29, f32[4,128]{1,0:T(4,128)} %bitcast.30, s32[4,128]{1,0:T(4,128)} %bitcast.31, bf16[128,3072]{1,0:T(8,128)(2,1)} %bitcast.23, ...), custom_call_target="tpu_custom_call" | custom-call | flops 7247757312 | bytes 16777216 | tf_op jit(solution)/shard_map/pallas_call | solution.py:379
  69.3 2.5 %shard_map.122 = (bf16[128,3072]{1,0:T(8,128)(2,1)}, bf16[3072,384]{1,0:T(8,128)(2,1)}, bf16[3072,384]{1,0:T(8,128)(2,1)}) custom-call(bf16[32,3072]{1,0:T(8,128)(2,1)S(1)} %get-tuple-element.10.packed_grad, f32[32,256]{1,0:T(8,128)S(1)} %get-tuple-element.11.tab, bf16[3072,384]{1,0:T(8,128)(2,1)S(1)} %get-tuple-element.12.dw_gate, ...), custom_call_target="tpu_custom_call" | custom-call | tf_op jit(solution)/shard_map/pallas_call | solution.py:434

commit v3 on v2

--- a/solution.py
+++ b/solution.py
@@ -81,8 +81,7 @@
         return copy
 
     barrier = pltpu.get_barrier_semaphore()
-    partners = [device(0, 1, 0), device(0, -1, 0), device(0, 0, 1)]
-    partners += [device(-1, 0, 0), device(1, 0, 0)]
+    partners = [device(0, 1, 0), device(0, -1, 0), device(0, 0, 1), device(1, 0, 0)]
     for partner in partners:
         pl.semaphore_signal(barrier, inc=1, device_id=partner, device_id_type=MESH)
 
@@ -128,17 +127,18 @@
 
     pl.semaphore_wait(barrier, len(partners))
 
-    def gather_hop(buf, src, dst, ss, rs, hop, waits):
+    def gather_hop(buf, src, dst, ss, rs, hop, waits, turns):
         copies = {}
-        for piece in range(PIECES):
+        for turn in turns:
+            if hop == 3 and turn >= PIECES // 2:
+                continue
             for way, by in enumerate((1, -1)):
-                if hop == 3 and (piece < PIECES // 2) != (way == 0):
-                    continue
                 if waits is not None:
-                    waits[way, piece].wait_recv()
+                    waits[way, turn].wait_recv()
+                piece = turn if way == 0 else PIECES - 1 - turn
                 lanes = slice(piece * PIECE, (piece + 1) * PIECE)
-                at = (way * 4 + hop) * PIECES + piece
-                copies[way, piece] = send(
+                at = (way * 4 + hop) * PIECES + turn
+                copies[way, turn] = send(
                     buf.at[src(hop, by), lanes],
                     buf.at[dst(hop, by), lanes],
                     ss.at[at],
@@ -147,23 +147,23 @@
                 )
         return copies
 
-    def now_hop(hop, waits):
+    def now_hop(hop, waits, turns=range(PIECES)):
         def src(hop, by):
             return place(-hop * by)
 
         def dst(hop, by):
             return place(-(hop + 1) * by)
 
-        return gather_hop(rows_now, src, dst, now_ss, now_rs, hop, waits)
+        return gather_hop(rows_now, src, dst, now_ss, now_rs, hop, waits, turns)
 
     def old_place(there):
         return pl.ds(pl.multiple_of(group(there, k) * CAP, CAP), CAP)
 
-    def old_hop(hop, waits):
+    def old_hop(hop, waits, turns=range(PIECES)):
         def both(hop, by):
             return old_place(chip(-hop * by))
 
-        return gather_hop(rows_old, both, both, old_ss, old_rs, hop, waits)
+        return gather_hop(rows_old, both, both, old_ss, old_rs, hop, waits, turns)
 
     def arrive(before, after):
         for key, copy in before.items():
@@ -207,7 +207,6 @@
         old_table.astype(BF16), x_old_v[...], preferred_element_type=F32
     ).astype(BF16)
 
-    old_0 = old_hop(0, None)
     share(0)
     now_1 = now_hop(1, now_0)
     for by in (2, -2):
@@ -246,13 +245,13 @@
             hidden_sent[by, core].wait_recv()
     for j in range(3):
         gate_step(NEAR, j)
-    now_3 = now_hop(3, now_2)
+    for way in range(2):
+        now_2[way, 0].wait_recv()
     send_hidden(4)
+    now_3 = now_hop(3, None)
+    old_0 = old_hop(0, None)
     for c in range(CHUNKS):
         term_step(NEAR, c)
-    old_1 = old_hop(1, old_0)
-    share(-1)
-    share(1)
 
     moving = {}
 
@@ -279,6 +278,14 @@
     def long_way(c):
         return 0 if c < CHUNKS // 2 else 1
 
+    def dw_step(i):
+        rows = slice(i * 256, (i + 1) * 256)
+        value = lax.dot_general(
+            rows_old[:, rows], old[...], (((0,), (0,)), ((), ())), preferred_element_type=F32
+        ).astype(BF16)
+        dw_gate[rows, :] = value[:, 0:WIDTH]
+        dw_up[rows, :] = value[:, WIDTH:BOTH]
+
     arrive(now_2, now_3)
     for copy in now_3.values():
         copy.wait_recv()
@@ -287,36 +294,32 @@
             hidden_sent[by, core].wait_recv()
     for j in range(3):
         gate_step(FAR, j)
-    for c in order:
-        term_step(FAR, c)
-        push(c, long_way(c), 0)
-        push(c, 1 - long_way(c), 1)
-    old_2 = old_hop(2, old_1)
+    old_1, old_2 = {}, {}
+    for turn in range(PIECES):
+        old_1 |= old_hop(1, old_0, [turn])
+        for c in order[2 * turn : 2 * turn + 2]:
+            term_step(FAR, c)
+            push(c, long_way(c), 0)
+            push(c, 1 - long_way(c), 1)
+    share(-1)
+    share(1)
+    send_o[...] = term[place(0), :].astype(BF16)
+    own = send(send_o, land_o, own_ss.at[0], own_rs.at[0], device(-1, 0, 0))
+    for turn in range(PIECES):
+        old_2 |= old_hop(2, old_1, [turn])
+        for c in order[2 * turn : 2 * turn + 2]:
+            push(c, long_way(c), 1)
+            push(c, 1 - long_way(c), 2)
     share(-2)
     share(2)
-    send_o[...] = term[place(0), :].astype(BF16)
-    own = send(send_o, land_o, own_ss.at[0], own_rs.at[0], device(-1, 0, 0))
-
-    def dw_step(i):
-        rows = slice(i * 256, (i + 1) * 256)
-        value = lax.dot_general(
-            rows_old[:, rows], old[...], (((0,), (0,)), ((), ())), preferred_element_type=F32
-        ).astype(BF16)
-        dw_gate[rows, :] = value[:, 0:WIDTH]
-        dw_up[rows, :] = value[:, WIDTH:BOTH]
-
-    for c in order:
-        push(c, long_way(c), 1)
-    for c in order:
-        push(c, 1 - long_way(c), 2)
     old_3 = old_hop(3, old_2)
-    arrive(old_2, old_3)
-    share(-3)
-    share(3)
     for c in order:
         push(c, long_way(c), 2)
     for c in order:
         push(c, 1 - long_way(c), 3)
+    arrive(old_2, old_3)
+    share(-3)
+    share(3)
     for copy in old_3.values():
         copy.wait_recv()
     share(4, 0, D // 2)
@@ -328,6 +331,8 @@
     for i in range(12):
         dw_step(i)
 
+    for copy in sent:
+        copy.wait_send()
     table_sent.wait_recv()
     own.wait_recv()
     scale = tab_in[:, TOK : TOK + 1]
@@ -341,8 +346,6 @@
             + land_l[3, :, lanes].astype(F32)
         )
         packed_grad[:, lanes] = (scale * total).astype(BF16)
-    for copy in sent:
-        copy.wait_send()
 
 
 def finish(packed_grad, tab, dw_gate, dw_up, out, out_gate, out_up, spread, sem):

time: 71.9 us -> 70.3 us (0.978)
  Pallas kernels: 71.1 us -> 69.5 us
    pallas_call x1, Pallas kernels: 68.6 us -> 67 us  [shards(): pl.pallas_call(kernel, out_shape=(pltpu.VMEM((CAP, D), BF16), pltpu.VMEM(...]
where the time goes in v3:
time: 70.3 us; the launch traced here: 70.2 us
  Pallas kernels  69.5 us (99%)
    pallas_call x1, Pallas kernels, shards(): pl.pallas_call(kernel, out_shape=(pltpu.VMEM((CAP, D), BF16), pltpu.VMEM(...  67 us
    pallas_call x1, Pallas kernels, shards(): pl.pallas_call(finish, out_shape=(jax.ShapeDtypeStruct((TOK, D), BF16), j...  2.47 us

profile of v3, /device:TPU:30, one launch (start us, length us, event | category | flops | bytes accessed | tf_op | source)
XLA Modules:
  0.0 70.2 jit_solution(15005158533244892177)
XLA Ops:
  0.6 67.0 %shard_map.121 = (bf16[32,3072]{1,0:T(8,128)(2,1)S(1)}, f32[32,256]{1,0:T(8,128)S(1)}, bf16[3072,384]{1,0:T(8,128)(2,1)S(1)}, bf16[3072,384]{1,0:T(8,128)(2,1)S(1)}) custom-call(s32[4,128]{1,0:T(4,128)} %bitcast.29, f32[4,128]{1,0:T(4,128)} %bitcast.30, s32[4,128]{1,0:T(4,128)} %bitcast.31, bf16[128,3072]{1,0:T(8,128)(2,1)} %bitcast.23, ...), custom_call_target="tpu_custom_call" | custom-call | flops 7247757312 | bytes 16777216 | tf_op jit(solution)/shard_map/pallas_call | solution.py:382
  67.7 2.5 %shard_map.122 = (bf16[128,3072]{1,0:T(8,128)(2,1)}, bf16[3072,384]{1,0:T(8,128)(2,1)}, bf16[3072,384]{1,0:T(8,128)(2,1)}) custom-call(bf16[32,3072]{1,0:T(8,128)(2,1)S(1)} %get-tuple-element.10.packed_grad, f32[32,256]{1,0:T(8,128)S(1)} %get-tuple-element.11.tab, bf16[3072,384]{1,0:T(8,128)(2,1)S(1)} %get-tuple-element.12.dw_gate, ...), custom_call_target="tpu_custom_call" | custom-call | tf_op jit(solution)/shard_map/pallas_call | solution.py:437

commit v4 on v3

--- a/solution.py
+++ b/solution.py
@@ -102,30 +102,30 @@
         return slice(at, at + CAP)
 
     get_now = [load(ids_now, ids_now_v), load(gates_now, gates_now_v), load(x_now, x_now_v)]
+    gate_place, up_place = columns(k * WIDTH, WIDTH), columns(BOTH + k * WIDTH, WIDTH)
+    hidden_sent = {}
+
+    def send_hidden(by):
+        there = chip(by)
+        for core in range(2):
+            at = (by % RING - 1) * 2 + core
+            hidden_sent[by, core] = send(
+                hidden.at[:, columns(group(there, core) * WIDTH, WIDTH)],
+                hid.at[place(-by), core * WIDTH : (core + 1) * WIDTH],
+                hid_ss.at[at],
+                hid_rs.at[at],
+                device(0, by, 0),
+            )
+
+    pl.semaphore_wait(barrier, len(partners))
+    for by in (1, -1):
+        send_hidden(by)
     for copy in get_now:
         copy.wait()
-    get_old = [load(ids_old, ids_old_v), load(x_old, x_old_v)]
-    gate_place, up_place = columns(k * WIDTH, WIDTH), columns(BOTH + k * WIDTH, WIDTH)
-    get_weights = [load(w_gate, wts.at[:, gate_place]), load(w_up, wts.at[:, up_place])]
-    get_hidden = [
-        load(
-            hidden.at[:, columns(group(z, core) * WIDTH, WIDTH)],
-            hid.at[place(0), core * WIDTH : (core + 1) * WIDTH],
-        )
-        for core in range(2)
-    ]
-    get_stored = [load(gate_old, old.at[:, 0:WIDTH]), load(up_old, old.at[:, WIDTH:BOTH])]
-
     table, hits = routing(ids_now_v[...], expert)
     rows_now[place(0), :] = jnp.dot(
         table.astype(BF16), x_now_v[...], preferred_element_type=F32
     ).astype(BF16)
-    weight = jnp.sum(gates_now_v[...] * hits, axis=0, keepdims=True)
-    coef = jnp.sum(table * weight, axis=1, keepdims=True)
-    tab_out[:, 0:TOK] = table
-    tab_out[:, TOK : 2 * TOK] = jnp.broadcast_to(coef, (CAP, TOK))
-
-    pl.semaphore_wait(barrier, len(partners))
 
     def gather_hop(buf, src, dst, ss, rs, hop, waits, turns):
         copies = {}
@@ -177,27 +177,27 @@
         at = len(siblings)
         siblings.append(send(block, block, sib_ss.at[at], sib_rs.at[at], device(0, 0, 1)))
 
-    hidden_sent = {}
-
-    def send_hidden(by):
-        there = chip(by)
-        for core in range(2):
-            at = (by % RING - 1) * 2 + core
-            hidden_sent[by, core] = send(
-                hidden.at[:, columns(group(there, core) * WIDTH, WIDTH)],
-                hid.at[place(-by), core * WIDTH : (core + 1) * WIDTH],
-                hid_ss.at[at],
-                hid_rs.at[at],
-                device(0, by, 0),
-            )
-
     now_0 = now_hop(0, None)
+    get_old = [load(ids_old, ids_old_v), load(x_old, x_old_v)]
+    get_weights = [load(w_gate, wts.at[:, gate_place]), load(w_up, wts.at[:, up_place])]
+    get_hidden = [
+        load(
+            hidden.at[:, columns(group(z, core) * WIDTH, WIDTH)],
+            hid.at[place(0), core * WIDTH : (core + 1) * WIDTH],
+        )
+        for core in range(2)
+    ]
+    get_stored = [load(gate_old, old.at[:, 0:WIDTH]), load(up_old, old.at[:, WIDTH:BOTH])]
+
     weights_sent = [
         send(w_gate, wts.at[:, gate_place], w_ss.at[0], w_rs.at[0], device(0, 0, 1)),
         send(w_up, wts.at[:, up_place], w_ss.at[1], w_rs.at[1], device(0, 0, 1)),
     ]
-    for by in (1, -1):
-        send_hidden(by)
+    weight = jnp.sum(gates_now_v[...] * hits, axis=0, keepdims=True)
+    coef = jnp.sum(table * weight, axis=1, keepdims=True)
+    tab_out[:, 0:TOK] = table
+    tab_out[:, TOK : 2 * TOK] = jnp.broadcast_to(coef, (CAP, TOK))
+
     table_sent = send(tab_out, tab_in, tab_ss.at[0], tab_rs.at[0], device(-1, 0, 0))
 
     for copy in get_old:
@@ -226,7 +226,7 @@
         gate = jnp.dot(rows_now[rows, :], wts[:, lanes], preferred_element_type=F32)
         up = jnp.dot(rows_now[rows, :], wts[:, up_lanes], preferred_element_type=F32)
         incoming = hid[rows, lanes].astype(F32)
-        sig = 1.0 / (1.0 + jnp.exp(-gate))
+        sig = jax.nn.sigmoid(gate)
         act = gate * sig
         slope = sig * (1.0 + gate * (1.0 - sig))
         grads[rows, lanes] = (incoming * up * slope).astype(BF16)

time: 70.3 us -> 70.9 us (level)
  no operation moved by 1% of the time
where the time goes in v4:
time: 70.9 us; the launch traced here: 70.6 us
  Pallas kernels  69.9 us (99%)
    pallas_call x1, Pallas kernels, shards(): pl.pallas_call(kernel, out_shape=(pltpu.VMEM((CAP, D), BF16), pltpu.VMEM(...  67.5 us
    pallas_call x1, Pallas kernels, shards(): pl.pallas_call(finish, out_shape=(jax.ShapeDtypeStruct((TOK, D), BF16), j...  2.47 us

profile of v4, /device:TPU:30, one launch (start us, length us, event | category | flops | bytes accessed | tf_op | source)
XLA Modules:
  0.0 70.6 jit_solution(2679248730267000687)
XLA Ops:
  0.6 67.5 %shard_map.121 = (bf16[32,3072]{1,0:T(8,128)(2,1)S(1)}, f32[32,256]{1,0:T(8,128)S(1)}, bf16[3072,384]{1,0:T(8,128)(2,1)S(1)}, bf16[3072,384]{1,0:T(8,128)(2,1)S(1)}) custom-call(s32[4,128]{1,0:T(4,128)} %bitcast.29, f32[4,128]{1,0:T(4,128)} %bitcast.30, s32[4,128]{1,0:T(4,128)} %bitcast.31, bf16[128,3072]{1,0:T(8,128)(2,1)} %bitcast.23, ...), custom_call_target="tpu_custom_call" | custom-call | flops 7247757312 | bytes 16777216 | tf_op jit(solution)/shard_map/pallas_call | solution.py:382
  68.1 2.5 %shard_map.122 = (bf16[128,3072]{1,0:T(8,128)(2,1)}, bf16[3072,384]{1,0:T(8,128)(2,1)}, bf16[3072,384]{1,0:T(8,128)(2,1)}) custom-call(bf16[32,3072]{1,0:T(8,128)(2,1)S(1)} %get-tuple-element.10.packed_grad, f32[32,256]{1,0:T(8,128)S(1)} %get-tuple-element.11.tab, bf16[3072,384]{1,0:T(8,128)(2,1)S(1)} %get-tuple-element.12.dw_gate, ...), custom_call_target="tpu_custom_call" | custom-call | tf_op jit(solution)/shard_map/pallas_call | solution.py:437

commit v5 on v3

--- a/solution.py
+++ b/solution.py
@@ -305,18 +305,27 @@
     share(1)
     send_o[...] = term[place(0), :].astype(BF16)
     own = send(send_o, land_o, own_ss.at[0], own_rs.at[0], device(-1, 0, 0))
-    for turn in range(PIECES):
-        old_2 |= old_hop(2, old_1, [turn])
+    def reduce_long(turn, hop):
         for c in order[2 * turn : 2 * turn + 2]:
-            push(c, long_way(c), 1)
-            push(c, 1 - long_way(c), 2)
+            push(c, long_way(c), hop)
+
+    def reduce_short(turn, hop):
+        for c in order[2 * turn : 2 * turn + 2]:
+            push(c, 1 - long_way(c), hop)
+
+    old_2 |= old_hop(2, old_1, [0])
+    reduce_short(0, 2)
+    reduce_long(0, 1)
+    old_2 |= old_hop(2, old_1, [1])
+    reduce_short(1, 2)
+    reduce_long(1, 1)
     share(-2)
     share(2)
+    reduce_short(0, 3)
     old_3 = old_hop(3, old_2)
-    for c in order:
-        push(c, long_way(c), 2)
-    for c in order:
-        push(c, 1 - long_way(c), 3)
+    reduce_long(0, 2)
+    reduce_short(1, 3)
+    reduce_long(1, 2)
     arrive(old_2, old_3)
     share(-3)
     share(3)
@@ -324,8 +333,8 @@
         copy.wait_recv()
     share(4, 0, D // 2)
     share(4, D // 2, D)
-    for c in order:
-        push(c, long_way(c), 3)
+    reduce_long(0, 3)
+    reduce_long(1, 3)
     for copy in siblings:
         copy.wait_recv()
     for i in range(12):

time: 70.3 us -> 71.1 us (1.011)
  no operation moved by 1% of the time
where the time goes in v5:
time: 71.1 us; the launch traced here: 70.5 us
  Pallas kernels  69.8 us (98%)
    pallas_call x1, Pallas kernels, shards(): pl.pallas_call(kernel, out_shape=(pltpu.VMEM((CAP, D), BF16), pltpu.VMEM(...  67.3 us
    pallas_call x1, Pallas kernels, shards(): pl.pallas_call(finish, out_shape=(jax.ShapeDtypeStruct((TOK, D), BF16), j...  2.47 us

profile of v5, /device:TPU:30, one launch (start us, length us, event | category | flops | bytes accessed | tf_op | source)
XLA Modules:
  0.0 70.5 jit_solution(17574650568211195449)
XLA Ops:
  0.6 67.3 %shard_map.121 = (bf16[32,3072]{1,0:T(8,128)(2,1)S(1)}, f32[32,256]{1,0:T(8,128)S(1)}, bf16[3072,384]{1,0:T(8,128)(2,1)S(1)}, bf16[3072,384]{1,0:T(8,128)(2,1)S(1)}) custom-call(s32[4,128]{1,0:T(4,128)} %bitcast.29, f32[4,128]{1,0:T(4,128)} %bitcast.30, s32[4,128]{1,0:T(4,128)} %bitcast.31, bf16[128,3072]{1,0:T(8,128)(2,1)} %bitcast.23, ...), custom_call_target="tpu_custom_call" | custom-call | flops 7247757312 | bytes 16777216 | tf_op jit(solution)/shard_map/pallas_call | solution.py:391
  68.0 2.5 %shard_map.122 = (bf16[128,3072]{1,0:T(8,128)(2,1)}, bf16[3072,384]{1,0:T(8,128)(2,1)}, bf16[3072,384]{1,0:T(8,128)(2,1)}) custom-call(bf16[32,3072]{1,0:T(8,128)(2,1)S(1)} %get-tuple-element.10.packed_grad, f32[32,256]{1,0:T(8,128)S(1)} %get-tuple-element.11.tab, bf16[3072,384]{1,0:T(8,128)(2,1)S(1)} %get-tuple-element.12.dw_gate, ...), custom_call_target="tpu_custom_call" | custom-call | tf_op jit(solution)/shard_map/pallas_call | solution.py:446
